TPU v7x, 128 devices: a whole 4x4x4 slice. The times are simulated.
128 devices in a mesh: grp: 8 (over x, core), mem: 16 (over z, y).
Axes of the slice: x: 4, y: 4, z: 4, core: 2. Of those that a mesh axis runs over, the one named last changes fastest.
Arguments:
- history: bfloat16 [65536, 256], P(('grp', 'mem')), may hold values from -6 to 6
- tiles: bfloat16 [81920, 128, 128], P(('grp', 'mem')), may hold values from -0.0390625 to 0.0390625
- tile_row: int32 [81920], P(('grp', 'mem')), may hold values from 0 to 63
- tile_col: int32 [81920], P(('grp', 'mem')), may hold values from 0 to 63
- weight: bfloat16 [256, 256], replicated, may hold values from -0.375 to 0.375
- bias: float32 [256], replicated, may hold values from -3 to 3
- cotangent: bfloat16 [65536, 256], P(('grp', 'mem')), may hold values from -0.0234375 to 0.0234375
Outputs:
- activation: bfloat16 [65536, 256], P(('grp', 'mem'))
- weight_grad: float32 [256, 256], replicated
- bias_grad: float32 [256], replicated
All inputs are finite; a program needn't handle non-finite values.
Results may differ from a plain program's by a relative error of at most 0.012.
Values may be sent and summed in bfloat16 or wider, within the bound.
A program may use at most 128 MiB of HBM per device.

v0:
```python
import math

import jax
import jax.numpy as jnp
from jax import lax
from jax.sharding import PartitionSpec as P


def per_device(history, tiles, tile_row, tile_col, weight, bias, cotangent):
    own_rows = history.shape[0]
    block = tiles.shape[1]
    width = history.shape[1]
    group = lax.all_gather(history, "mem", axis=0, tiled=True)
    nblk = group.shape[0] // block
    flat_blocks = group.reshape(nblk, block * width)
    step = math.gcd(tiles.shape[0], 64)
    count = tiles.shape[0] // step
    block_ids = lax.broadcasted_iota(jnp.int32, (step, nblk), 1)

    def accumulate(index, dense):
        start = index * step
        piece = lax.dynamic_slice_in_dim(tiles, start, step, 0)
        rows = lax.dynamic_slice_in_dim(tile_row, start, step, 0)
        cols = lax.dynamic_slice_in_dim(tile_col, start, step, 0)
        col_table = (cols[:, None] == block_ids).astype(jnp.bfloat16)
        row_table = (rows[:, None] == block_ids).astype(jnp.bfloat16)
        picked = jnp.dot(col_table, flat_blocks, preferred_element_type=jnp.float32).astype(
            jnp.bfloat16
        )
        picked = picked.reshape(step, block, width)
        part = jnp.einsum("tij,tjh->tih", piece, picked, preferred_element_type=jnp.float32)
        part = part.reshape(step, block * width)
        upper = part.astype(jnp.bfloat16)
        lower = (part - upper.astype(jnp.float32)).astype(jnp.bfloat16)
        contract = (((0,), (0,)), ((), ()))
        added = lax.dot_general(row_table, upper, contract, preferred_element_type=jnp.float32)
        added = added + lax.dot_general(
            row_table, lower, contract, preferred_element_type=jnp.float32
        )
        return dense + added

    dense = lax.fori_loop(0, count, accumulate, jnp.zeros((nblk, block * width), jnp.float32))
    flat = dense.reshape(nblk * block, width)
    total = lax.psum(flat, "mem")
    summed = lax.dynamic_slice_in_dim(total, lax.axis_index("mem") * own_rows, own_rows, 0)
    merged = summed.astype(jnp.bfloat16)
    pre = jnp.dot(merged, weight, preferred_element_type=jnp.float32) + bias
    sig = jax.nn.sigmoid(pre)
    activation = (pre * sig).astype(jnp.bfloat16)
    slope = sig * (1.0 + pre * (1.0 - sig))
    masked = (cotangent.astype(jnp.float32) * slope).astype(jnp.bfloat16)
    local_grad = lax.dot_general(
        merged, masked, (((0,), (0,)), ((), ())), preferred_element_type=jnp.float32
    )
    local_bias = jnp.sum(masked.astype(jnp.float32), axis=0)
    weight_grad, bias_grad = lax.psum((local_grad, local_bias), ("grp", "mem"))
    return (activation, weight_grad, bias_grad)


def solution(mesh):
    placed = (
        P(("grp", "mem"), None),
        P(("grp", "mem"), None, None),
        P(("grp", "mem")),
        P(("grp", "mem")),
        P(),
        P(),
        P(("grp", "mem"), None),
    )
    return jax.shard_map(
        per_device,
        mesh=mesh,
        in_specs=placed,
        out_specs=(P(("grp", "mem"), None), P(), P()),
        check_vma=False,
    )
```

profile of v0, /device:TPU:1, one launch (start us, length us, event | category | flops | bytes accessed | tf_op | source)
XLA Modules:
  0.0 768.6 jit_solution(8757463280255203466)
XLA Ops:
  8.0 57.1 %all-gather.2.cloned.1.call-done = bf16[8192,256]{1,0:T(8,128)(2,1)} async-done(((bf16[512,256]{1,0:T(8,128)(2,1)}), bf16[8192,256]{1,0:T(8,128)(2,1)}) %all-gather.2.cloned.1.call-update) | async-done | bytes 4194320 | tf_op jit(solution)/shard_map/all_gather | solution.py:13
  65.1 7.4 reshape.29
  72.5 345.5 %while.15 = (s32[]{:T(128)}, f32[64,32768]{1,0:T(8,128)}, s32[640]{0:T(1024)}, bf16[640,128,128]{2,1,0:T(8,128)(2,1)}, s32[640]{0:T(1024)}, /*index=5*/bf16[64,3...) while((s32[]{:T(128)}, f32[64,32768]{1,0:T(8,128)}, s32[640]{0:T(1024)}, ...), condition=%wide.region_1.0_spmd.clone.clone, body=%wide.region_0.0_spmd.clone.clone.sunk | while | flops 1361063936 | bytes 132122568 | solution.py:42
  86.2 4.9 fusion.31
  91.1 13.7 %fusion.32 = f32[64,32768]{1,0:T(8,128)} fusion(f32[64,32768]{1,0:T(8,128)} %fusion.31, f32[64,32768]{1,0:T(8,128)} %get-tuple-element.235, f32[64,32768]{1,0:T(8,128)} %bitcast.21, pred[]{:T(512)S(6)} %compare.3, s32[64]{0:T(128)S(1)} %dynamic_slice.43), kind=kOutput, calls=%fused_computation.2.clone.1 | convolution fusion | flops 283119616 | bytes 33554688 | tf_op jit(solution)/shard_map/while/body/eval_jaxpr/dot_general | solution.py:37
  118.6 4.9 fusion.31
  123.5 16.1 %fusion.32 = f32[64,32768]{1,0:T(8,128)} fusion(f32[64,32768]{1,0:T(8,128)} %fusion.31, f32[64,32768]{1,0:T(8,128)} %get-tuple-element.235, f32[64,32768]{1,0:T(8,128)} %bitcast.21, pred[]{:T(512)S(6)} %compare.3, s32[64]{0:T(128)S(1)} %dynamic_slice.43), kind=kOutput, calls=%fused_computation.2.clone.1 | convolution fusion | flops 283119616 | bytes 33554688 | tf_op jit(solution)/shard_map/while/body/eval_jaxpr/dot_general | solution.py:37
  153.4 4.9 fusion.31
  158.3 16.1 %fusion.32 = f32[64,32768]{1,0:T(8,128)} fusion(f32[64,32768]{1,0:T(8,128)} %fusion.31, f32[64,32768]{1,0:T(8,128)} %get-tuple-element.235, f32[64,32768]{1,0:T(8,128)} %bitcast.21, pred[]{:T(512)S(6)} %compare.3, s32[64]{0:T(128)S(1)} %dynamic_slice.43), kind=kOutput, calls=%fused_computation.2.clone.1 | convolution fusion | flops 283119616 | bytes 33554688 | tf_op jit(solution)/shard_map/while/body/eval_jaxpr/dot_general | solution.py:37
  188.2 4.9 fusion.31
  193.1 16.1 %fusion.32 = f32[64,32768]{1,0:T(8,128)} fusion(f32[64,32768]{1,0:T(8,128)} %fusion.31, f32[64,32768]{1,0:T(8,128)} %get-tuple-element.235, f32[64,32768]{1,0:T(8,128)} %bitcast.21, pred[]{:T(512)S(6)} %compare.3, s32[64]{0:T(128)S(1)} %dynamic_slice.43), kind=kOutput, calls=%fused_computation.2.clone.1 | convolution fusion | flops 283119616 | bytes 33554688 | tf_op jit(solution)/shard_map/while/body/eval_jaxpr/dot_general | solution.py:37
  223.0 4.9 fusion.31
  227.9 16.1 %fusion.32 = f32[64,32768]{1,0:T(8,128)} fusion(f32[64,32768]{1,0:T(8,128)} %fusion.31, f32[64,32768]{1,0:T(8,128)} %get-tuple-element.235, f32[64,32768]{1,0:T(8,128)} %bitcast.21, pred[]{:T(512)S(6)} %compare.3, s32[64]{0:T(128)S(1)} %dynamic_slice.43), kind=kOutput, calls=%fused_computation.2.clone.1 | convolution fusion | flops 283119616 | bytes 33554688 | tf_op jit(solution)/shard_map/while/body/eval_jaxpr/dot_general | solution.py:37
  257.8 4.9 fusion.31
  262.7 16.1 %fusion.32 = f32[64,32768]{1,0:T(8,128)} fusion(f32[64,32768]{1,0:T(8,128)} %fusion.31, f32[64,32768]{1,0:T(8,128)} %get-tuple-element.235, f32[64,32768]{1,0:T(8,128)} %bitcast.21, pred[]{:T(512)S(6)} %compare.3, s32[64]{0:T(128)S(1)} %dynamic_slice.43), kind=kOutput, calls=%fused_computation.2.clone.1 | convolution fusion | flops 283119616 | bytes 33554688 | tf_op jit(solution)/shard_map/while/body/eval_jaxpr/dot_general | solution.py:37
  292.6 4.9 fusion.31
  297.5 16.1 %fusion.32 = f32[64,32768]{1,0:T(8,128)} fusion(f32[64,32768]{1,0:T(8,128)} %fusion.31, f32[64,32768]{1,0:T(8,128)} %get-tuple-element.235, f32[64,32768]{1,0:T(8,128)} %bitcast.21, pred[]{:T(512)S(6)} %compare.3, s32[64]{0:T(128)S(1)} %dynamic_slice.43), kind=kOutput, calls=%fused_computation.2.clone.1 | convolution fusion | flops 283119616 | bytes 33554688 | tf_op jit(solution)/shard_map/while/body/eval_jaxpr/dot_general | solution.py:37
  332.3 16.1 %fusion.32 = f32[64,32768]{1,0:T(8,128)} fusion(f32[64,32768]{1,0:T(8,128)} %fusion.31, f32[64,32768]{1,0:T(8,128)} %get-tuple-element.235, f32[64,32768]{1,0:T(8,128)} %bitcast.21, pred[]{:T(512)S(6)} %compare.3, s32[64]{0:T(128)S(1)} %dynamic_slice.43), kind=kOutput, calls=%fused_computation.2.clone.1 | convolution fusion | flops 283119616 | bytes 33554688 | tf_op jit(solution)/shard_map/while/body/eval_jaxpr/dot_general | solution.py:37
  367.1 16.1 %fusion.32 = f32[64,32768]{1,0:T(8,128)} fusion(f32[64,32768]{1,0:T(8,128)} %fusion.31, f32[64,32768]{1,0:T(8,128)} %get-tuple-element.235, f32[64,32768]{1,0:T(8,128)} %bitcast.21, pred[]{:T(512)S(6)} %compare.3, s32[64]{0:T(128)S(1)} %dynamic_slice.43), kind=kOutput, calls=%fused_computation.2.clone.1 | convolution fusion | flops 283119616 | bytes 33554688 | tf_op jit(solution)/shard_map/while/body/eval_jaxpr/dot_general | solution.py:37
  401.8 16.1 %fusion.32 = f32[64,32768]{1,0:T(8,128)} fusion(f32[64,32768]{1,0:T(8,128)} %fusion.31, f32[64,32768]{1,0:T(8,128)} %get-tuple-element.235, f32[64,32768]{1,0:T(8,128)} %bitcast.21, pred[]{:T(512)S(6)} %compare.3, s32[64]{0:T(128)S(1)} %dynamic_slice.43), kind=kOutput, calls=%fused_computation.2.clone.1 | convolution fusion | flops 283119616 | bytes 33554688 | tf_op jit(solution)/shard_map/while/body/eval_jaxpr/dot_general | solution.py:37
  418.0 9.3 %reshape.30 = f32[8192,256]{1,0:T(8,128)} reshape(f32[64,32768]{1,0:T(8,128)} %get-tuple-element.130) | data formatting | bytes 16777216 | tf_op jit(solution)/shard_map/reshape | solution.py:43
  427.2 185.0 %all-reduce.4 = bf16[8192,256]{1,0:T(8,128)(2,1)} all-reduce(f32[8192,256]{1,0:T(8,128)} %reshape.30), channel_id=1, replica_groups=mesh['grp'=8,'mem'=16] {'mem'}, use_global_device_ids=true, to_apply=%region_2.0 | all-reduce | flops 2097152 | bytes 12582912 | tf_op jit(solution)/shard_map/psum | solution.py:44
  616.2 67.6 %psum.23 = f32[256]{0:T(256)} all-reduce(f32[256]{0:T(256)S(1)} %get-tuple-element.184), channel_id=1, replica_groups=mesh['grp'=8,'mem'=16] {'grp','mem'}, use_global_device_ids=true, to_apply=%region_5.0 | all-reduce | flops 256 | bytes 2048 | tf_op jit(solution)/shard_map/psum | solution.py:56
  683.8 76.3 %all-reduce.3.cloned.1.call-done = f32[256,256]{1,0:T(8,128)} async-done(((f32[256,256]{1,0:T(8,128)}), f32[256,256]{1,0:T(8,128)}) %all-reduce.3.cloned.1.call-update) | async-done | bytes 262160 | tf_op jit(solution)/shard_map/psum | solution.py:56
  (97 shorter events, 158.5 us)
Async XLA Ops:
  7.2 605.0 %copy-start = (bf16[256,256]{1,0:T(8,128)(2,1)S(1)}, bf16[256,256]{1,0:T(8,128)(2,1)}, u32[]{:S(2)}) copy-start(bf16[256,256]{1,0:T(8,128)(2,1)} %param.13) | copy-start | bytes 393220
  7.2 57.9 %all-gather.2.cloned.1.call-start = ((), (), s32[]{:S(2)}) async-start(), calls=%async_computation | async-start | bytes 4456448 | tf_op jit(solution)/shard_map/all_gather | solution.py:13
  7.9 752.2 %all-reduce.3.cloned.1.call-start = ((), (), s32[]{:S(2)}) async-start(), calls=%async_computation.1 | async-start | bytes 524288 | tf_op jit(solution)/shard_map/psum | solution.py:56
  85.4 5.7 copy-start.1
  117.8 5.7 copy-start.1
  152.6 5.7 copy-start.1
  187.4 5.7 copy-start.1
  222.2 5.7 copy-start.1
  257.0 5.7 copy-start.1
  291.8 5.7 copy-start.1
  326.5 5.7 copy-start.1
  361.3 5.7 copy-start.1
  396.1 5.7 copy-start.1
  427.2 185.0 %copy-start.2 = (bf16[512,256]{1,0:T(8,128)(2,1)S(1)}, bf16[512,256]{1,0:T(8,128)(2,1)}, u32[]{:S(2)}) copy-start(bf16[512,256]{1,0:T(8,128)(2,1)} %param.15) | copy-start | bytes 786436
  427.2 185.0 %copy-start.3 = (f32[256]{0:T(256)S(1)}, f32[256]{0:T(256)}, u32[]{:S(2)}) copy-start(f32[256]{0:T(256)} %param.14) | copy-start | bytes 3076
Sparse Core Ops, SparseCore 0:
  10.2 54.8 all-gather.1
  616.3 143.7 all-reduce.2
where the time goes:
time: 771 us; the launch traced here: 769 us
  matrix products  275 us (36%)
  blocking collectives  253 us (33%)
  waiting for transfers between devices  134 us (17%)
  local copies, waits for them, and re-layouts  92.5 us (12%)
  between operations  14.1 us (2%)
    psum x1, blocking collectives, per_device(): total = lax.psum(flat, 'mem')  185 us
    dot_general x10, matrix products, accumulate(): lax.dot_general(row_table, lower, contract, preferred_element_type=jnp.fl...  159 us
    psum x1, waiting for transfers between devices, per_device(): weight_grad, bias_grad = lax.psum((local_grad, local_bias), ('grp', 'mem'))  76.3 us
    psum x1, blocking collectives, per_device(): weight_grad, bias_grad = lax.psum((local_grad, local_bias), ('grp', 'mem'))  67.6 us
    while x40, local copies, waits for them, and re-layouts  58.4 us
    all_gather x1, waiting for transfers between devices, per_device(): group = lax.all_gather(history, 'mem', axis=0, tiled=True)  57.1 us
    dot_general x10, matrix products, accumulate(): lax.dot_general(row_table, upper, contract, preferred_element_type=jnp.fl...  49 us
    dot_general x10, matrix products, accumulate(): jnp.dot(col_table, flat_blocks, preferred_element_type=jnp.float32)  34.7 us
  transfers between devices with their start and end apart: 2, of which 2 were waited for; matrix products, arithmetic and copies ran while one was open for 0% of the time, Pallas kernels for 0%

commit v1 on v0

v1 whole, which is shorter than its diff:
```python
import functools

import jax
import jax.numpy as jnp
from jax import lax
from jax.experimental import pallas as pl
from jax.experimental.pallas import tpu as pltpu
from jax.sharding import PartitionSpec as P

MESH = pl.DeviceIdType.MESH
SIDE = 4
MEM = SIDE * SIDE
GRP = 8
OWN = 4
BS = 128
H = 256
NBLK = MEM * OWN
TILES = 640
PAIRS = (TILES + NBLK) // 2
LANES = 768
UNROLL = 32
PIECE = H // MEM
WIDE = H + 128
BF16 = jnp.bfloat16
F32 = jnp.float32
I32 = jnp.int32


def matched(j):
    return -1 if j % 2 == 0 else 1


def wrap(d):
    d = d % SIDE
    return -1 if d == SIDE - 1 else d


def parent(j, df, ds):
    axis, d = (1, ds) if ds != 0 else (0, df)
    return axis, (matched(j) if d == 2 else d)


def children(j, df, ds):
    m = matched(j)
    if ds != 0:
        return [(1, -m)] if ds == m else []
    kids = [(1, 1), (1, -1)]
    if df == 0:
        kids += [(0, 1), (0, -1)]
    elif df == m:
        kids += [(0, -m)]
    return kids


SLOT = {}
for _j in range(OWN):
    for _df in (0, 1, -1, 2):
        for _ds in (0, 1, -1, 2):
            for _c in children(_j, _df, _ds):
                SLOT[(_j, _df, _ds) + _c] = len(SLOT)
NSEND = len(SLOT)


def sort_tiles(row, col, order, ends):
    r_sub = lax.broadcasted_iota(I32, (NBLK, TILES), 0)
    count = jnp.sum(jnp.where(r_sub == row, 1, 0), axis=1, keepdims=True)
    pairs = (count + 1) // 2
    before = lax.broadcasted_iota(I32, (NBLK, 128), 0)
    here = lax.broadcasted_iota(I32, (NBLK, 128), 1)
    start = jnp.sum(jnp.where(before < here, pairs, 0), axis=0, keepdims=True)
    mine = jnp.sum(jnp.where(before == here, pairs, 0), axis=0, keepdims=True)
    ends[0:1, :] = jnp.clip(jnp.where(mine > 0, start + mine - 1, PAIRS), 0, PAIRS)
    lane = lax.broadcasted_iota(I32, (128, 128), 1)
    sub = lax.broadcasted_iota(I32, (128, 128), 0)
    place = lax.broadcasted_iota(I32, (128, LANES), 1)
    other = lax.broadcasted_iota(I32, (128, TILES), 1)
    tile_at = jnp.zeros((1, LANES), I32)
    col_at = jnp.zeros((1, LANES), I32)
    first_at = jnp.zeros((1, LANES), I32)
    for a in range(TILES // 128):
        part = slice(a * 128, (a + 1) * 128)
        turn = lambda v: jnp.sum(jnp.where(lane == sub, v[:, part], 0), axis=1, keepdims=True)
        row_c = turn(row)
        col_c = turn(col)
        number = sub[:, 0:1] + a * 128
        rank = jnp.sum(
            jnp.where((row == row_c) & (other < number), 1, 0), axis=1, keepdims=True
        )
        begin = jnp.sum(jnp.where(lane == row_c, start, 0), axis=1, keepdims=True)
        at = place == 2 * begin + rank
        tile_at += jnp.sum(jnp.where(at, TILES - number, 0), axis=0, keepdims=True)
        col_at += jnp.sum(jnp.where(at, col_c, 0), axis=0, keepdims=True)
        first_at += jnp.sum(jnp.where(at & (rank == 0), 1, 0), axis=0, keepdims=True)
    order[0:1, :] = jnp.clip(TILES - tile_at, 0, TILES)
    order[1:2, :] = jnp.clip(col_at, 0, NBLK - 1)
    order[2:3, :] = 1 - first_at


def kernel(
    hist, tiles, row, col, weight, bias, cot,
    act, wgrad, bgrad,
    hbuf, tbuf, pbuf, acc, rbuf, order_v, ends_v, order_s, ends_s,
    w_v, cot_v, gsend, got1, send2, got2, got3,
    local_sem, s_gather, r_gather, s_sum, r_sum, s_1, r_1, s_2, r_2, s_3, r_3,
):
    me = lax.axis_index("mem")
    grp = lax.axis_index("grp")
    z, y = me // SIDE, lax.rem(me, SIDE)

    def mem_id(dz, dy):
        return lax.rem(z + dz + SIDE, SIDE) * SIDE + lax.rem(y + dy + SIDE, SIDE)

    def device(j, df, ds):
        return mem_id(ds, df) if j < 2 else mem_id(df, ds)

    def block(j, df, ds):
        return device(j, df, ds) * OWN + j

    def neighbour(j, axis, side):
        return device(j, side, 0) if axis == 0 else device(j, 0, side)

    mem_others = [lax.rem(me + k, MEM) for k in range(1, MEM)]
    grp_others = [lax.rem(grp + k, GRP) for k in range(1, GRP)]

    load_tiles = pltpu.make_async_copy(tiles, tbuf.at[pl.ds(0, TILES)], local_sem.at[0])
    load_w = pltpu.make_async_copy(weight, w_v, local_sem.at[1])
    load_cot = pltpu.make_async_copy(cot, cot_v, local_sem.at[2])
    keep = [
        pltpu.make_async_copy(hist.at[j], hbuf.at[me * OWN + j], local_sem.at[3 + j])
        for j in range(OWN)
    ]

    barrier = pltpu.get_barrier_semaphore()
    for o in mem_others:
        pl.semaphore_signal(barrier, inc=1, device_id={"mem": o}, device_id_type=MESH)
    for o in grp_others:
        pl.semaphore_signal(barrier, inc=1, device_id={"grp": o}, device_id_type=MESH)
    pl.semaphore_wait(barrier, MEM - 1 + GRP - 1)

    sends = []

    def send(j, df, ds, axis, side):
        b = block(j, df, ds)
        copy = pltpu.make_async_remote_copy(
            src_ref=hist.at[j] if df == 0 and ds == 0 else hbuf.at[b],
            dst_ref=hbuf.at[b],
            send_sem=s_gather.at[len(sends)],
            recv_sem=r_gather.at[b],
            device_id={"mem": neighbour(j, axis, side)},
            device_id_type=MESH,
        )
        copy.start()
        sends.append(copy)

    def arrive(j, df, ds):
        b = block(j, df, ds)
        axis, side = parent(j, df, ds)
        pltpu.make_async_remote_copy(
            src_ref=hbuf.at[b],
            dst_ref=hbuf.at[b],
            send_sem=s_gather.at[0],
            recv_sem=r_gather.at[b],
            device_id={"mem": neighbour(j, axis, side)},
            device_id_type=MESH,
        ).wait_recv()

    def pass_on(j, df, ds):
        kids = children(j, df, ds)
        for axis, side in sorted(kids):
            send(j, df, ds, axis, side)

    for part in (0, 1):
        for j in range(OWN):
            send(j, 0, 0, 0, -matched(j) if part == 0 else matched(j))
    for j in range(OWN):
        for side in (1, -1):
            send(j, 0, 0, 1, side)
    for c in keep:
        c.start()
    load_tiles.start()
    load_w.start()
    load_cot.start()

    for j in range(OWN):
        arrive(j, matched(j), 0)
        pass_on(j, matched(j), 0)
    for j in range(OWN):
        arrive(j, -matched(j), 0)
        pass_on(j, -matched(j), 0)

    sort_tiles(row[...], col[...], order_v, ends_v)
    to_s = [
        pltpu.make_async_copy(order_v, order_s, local_sem.at[7]),
        pltpu.make_async_copy(ends_v, ends_s, local_sem.at[8]),
    ]
    for c in to_s:
        c.start()

    for j in range(OWN):
        arrive(j, 0, matched(j))
        pass_on(j, 0, matched(j))
    for j in range(OWN):
        arrive(j, 2, 0)
        pass_on(j, 2, 0)
    for df in (1, -1, 2):
        for j in range(OWN):
            arrive(j, df, matched(j))
            pass_on(j, df, matched(j))
    tbuf[TILES] = jnp.zeros((BS, BS), BF16)
    pbuf[PAIRS] = jnp.zeros((BS, H), BF16)
    acc[...] = jnp.zeros((BS, H), F32)
    load_tiles.wait()
    load_w.wait()
    load_cot.wait()
    for c in keep:
        c.wait()
    for c in to_s:
        c.wait()
    for df in (0, 1, -1, 2):
        for j in range(OWN):
            arrive(j, df, -matched(j))
    for df in (0, 1, -1, 2):
        for j in range(OWN):
            arrive(j, df, 2)
    for c in sends:
        c.wait_send()

    def product(slot):
        left = [tbuf[order_s[0, 2 * slot + k]] for k in (0, 1)]
        right = [hbuf[order_s[1, 2 * slot + k]] for k in (0, 1)]
        return jnp.dot(
            jnp.concatenate(left, axis=1),
            jnp.concatenate(right, axis=0),
            preferred_element_type=F32,
        )

    def batch(q, _):
        parts = [product(q * UNROLL + u) for u in range(UNROLL)]
        total = acc[...]
        for u in range(UNROLL):
            slot = q * UNROLL + u
            total = parts[u] + total * order_s[2, 2 * slot].astype(F32)
            pbuf[slot] = total.astype(BF16)
        acc[...] = total
        return 0

    lax.fori_loop(0, PAIRS // UNROLL, batch, 0)

    own = hbuf
    sums = []

    def reduce_block(j, df, ds):
        b = block(j, df, ds)
        kids = children(j, df, ds)
        partial = pbuf[ends_s[0, b]]
        if kids:
            total = partial.astype(F32)
            for axis, side in kids:
                slot = SLOT[(j, df, ds, axis, side)]
                pltpu.make_async_remote_copy(
                    src_ref=own.at[b],
                    dst_ref=rbuf.at[slot],
                    send_sem=s_sum.at[0],
                    recv_sem=r_sum.at[slot],
                    device_id={"mem": neighbour(j, axis, side)},
                    device_id_type=MESH,
                ).wait_recv()
                total = total + rbuf[slot].astype(F32)
            if df == 0 and ds == 0:
                return total
            partial = total.astype(BF16)
        own[b] = partial
        axis, side = parent(j, df, ds)
        there = (df, wrap(ds - side)) if axis == 1 else (wrap(df - side), ds)
        slot = SLOT[(j,) + there + (axis, -side)]
        copy = pltpu.make_async_remote_copy(
            src_ref=own.at[b],
            dst_ref=rbuf.at[slot],
            send_sem=s_sum.at[len(sums)],
            recv_sem=r_sum.at[slot],
            device_id={"mem": neighbour(j, axis, side)},
            device_id_type=MESH,
        )
        copy.start()
        sums.append(copy)

    for df in (2, 1, -1, 0):
        for j in range(OWN):
            reduce_block(j, df, 2)
    for df in (2, 1, -1, 0):
        for j in range(OWN):
            reduce_block(j, df, -matched(j))
    for df in (2, 1, -1, 0):
        for j in range(OWN):
            reduce_block(j, df, matched(j))
    for j in range(OWN):
        reduce_block(j, 2, 0)
    for j in range(OWN):
        reduce_block(j, -matched(j), 0)
    for j in range(OWN):
        reduce_block(j, matched(j), 0)

    grad_sum = jnp.zeros((H, H), F32)
    bias_sum = jnp.zeros((1, H), F32)
    for j in range(OWN):
        merged = reduce_block(j, 0, 0).astype(BF16)
        pre = jnp.dot(merged, w_v[...], preferred_element_type=F32) + bias[...]
        sig = jax.nn.sigmoid(pre)
        nodes = slice(j * BS, (j + 1) * BS)
        act[nodes, :] = (pre * sig).astype(BF16)
        slope = sig * (1.0 + pre * (1.0 - sig))
        masked = (cot_v[nodes, :].astype(F32) * slope).astype(BF16)
        grad_sum = grad_sum + lax.dot_general(
            merged, masked, (((0,), (0,)), ((), ())), preferred_element_type=F32
        )
        bias_sum = bias_sum + jnp.sum(masked.astype(F32), axis=0, keepdims=True)

    line = lax.broadcasted_iota(I32, (PIECE, 128), 0)
    beside = jnp.where(
        line == 0, bias_sum[:, 0:128], jnp.where(line == 1, bias_sum[:, 128:256], 0.0)
    ).astype(BF16)
    for m in range(MEM):
        gsend[m, :, 0:H] = grad_sum[m * PIECE : (m + 1) * PIECE, :].astype(BF16)
        gsend[m, :, H:WIDE] = beside

    def to_mem(src, dst, s, r, k):
        return pltpu.make_async_remote_copy(
            src_ref=src, dst_ref=dst, send_sem=s.at[k], recv_sem=r.at[k],
            device_id={"mem": mem_others[k]}, device_id_type=MESH,
        )

    first = [to_mem(gsend.at[o], got1.at[me], s_1, r_1, k) for k, o in enumerate(mem_others)]
    for c in first:
        c.start()
    got1[me] = gsend[me]
    for c in first:
        c.wait_recv()
    total = got1[0].astype(F32)
    for m in range(1, MEM):
        total = total + got1[m].astype(F32)
    send2[...] = total.astype(BF16)
    second = [
        pltpu.make_async_remote_copy(
            src_ref=send2, dst_ref=got2.at[grp], send_sem=s_2.at[k], recv_sem=r_2.at[k],
            device_id={"grp": o}, device_id_type=MESH,
        )
        for k, o in enumerate(grp_others)
    ]
    for c in second:
        c.start()
    got2[grp] = send2[...]
    for c in second:
        c.wait_recv()
    total = got2[0].astype(F32)
    for g in range(1, GRP):
        total = total + got2[g].astype(F32)
    got3[me] = total[:, 0:H].astype(BF16)
    third = [to_mem(got3.at[me], got3.at[me], s_3, r_3, k) for k in range(MEM - 1)]
    for c in third:
        c.start()
    bgrad[:, 0:128] = total[0:1, H:WIDE]
    bgrad[:, 128:256] = total[1:2, H:WIDE]
    for c in sums + first + second:
        c.wait_send()
    for c in third:
        c.wait_recv()
    for m in range(MEM):
        wgrad[m * PIECE : (m + 1) * PIECE, :] = got3[m].astype(F32)
    for c in third:
        c.wait_send()


def per_device(history, tiles, tile_row, tile_col, weight, bias, cotangent):
    any_ref = pl.BlockSpec(memory_space=pl.ANY)
    vmem = pl.BlockSpec(memory_space=pltpu.VMEM)
    dma = pltpu.SemaphoreType.DMA
    nodes = history.shape[0]
    act, wgrad, bgrad = pl.pallas_call(
        kernel,
        out_shape=(
            jax.ShapeDtypeStruct((nodes, H), BF16),
            jax.ShapeDtypeStruct((H, H), F32),
            jax.ShapeDtypeStruct((1, H), F32),
        ),
        in_specs=[any_ref, any_ref, vmem, vmem, any_ref, vmem, any_ref],
        out_specs=(vmem, vmem, vmem),
        scratch_shapes=[
            pltpu.VMEM((NBLK, BS, H), BF16),
            pltpu.VMEM((TILES + 1, BS, BS), BF16),
            pltpu.VMEM((PAIRS + 1, BS, H), BF16),
            pltpu.VMEM((BS, H), F32),
            pltpu.VMEM((NSEND, BS, H), BF16),
            pltpu.VMEM((8, LANES), I32),
            pltpu.VMEM((8, 128), I32),
            pltpu.SMEM((8, LANES), I32),
            pltpu.SMEM((8, 128), I32),
            pltpu.VMEM((H, H), BF16),
            pltpu.VMEM((OWN * BS, H), BF16),
                pltpu.VMEM((MEM, PIECE, WIDE), BF16),
            pltpu.VMEM((MEM, PIECE, WIDE), BF16),
            pltpu.VMEM((PIECE, WIDE), BF16),
            pltpu.VMEM((GRP, PIECE, WIDE), BF16),
            pltpu.VMEM((MEM, PIECE, H), BF16),
            dma((9,)),
            dma((NSEND,)),
            dma((NBLK,)),
            dma((NSEND,)),
            dma((NSEND,)),
            dma((MEM - 1,)),
            dma((MEM - 1,)),
            dma((GRP - 1,)),
            dma((GRP - 1,)),
            dma((MEM - 1,)),
            dma((MEM - 1,)),
        ],
        compiler_params=pltpu.CompilerParams(
            collective_id=0, has_side_effects=True, vmem_limit_bytes=61 * 2**20
        ),
    )(
        history.reshape(OWN, BS, H),
        tiles,
        tile_row.reshape(1, TILES),
        tile_col.reshape(1, TILES),
        weight,
        bias.reshape(1, H),
        cotangent,
    )
    return act, wgrad, bgrad.reshape(H)


def solution(mesh):
    both = ("grp", "mem")
    placed = (
        P(both, None),
        P(both, None, None),
        P(both),
        P(both),
        P(),
        P(),
        P(both, None),
    )
    return jax.shard_map(
        per_device,
        mesh=mesh,
        in_specs=placed,
        out_specs=(P(both, None), P(), P()),
        check_vma=False,
    )
```

time: 771 us -> 93.9 us (0.12)
  matrix products: 275 us -> 0 us
  blocking collectives: 253 us -> 0 us
  waiting for transfers between devices: 134 us -> 0 us
  Pallas kernels: 0 us -> 85.9 us
  local copies, waits for them, and re-layouts: 92.5 us -> 7.07 us
  between operations: 14.1 us -> 0.64 us
    dot_general x42 -> x0, matrix products: 275 us -> none  [the longest x10 159 us: accumulate(): lax.dot_general(row_table, lower, contract, preferred_element_type=jnp.fl...]
    psum x2 -> x0, blocking collectives: 253 us -> none  [the longest x1 185 us: per_device(): total = lax.psum(flat, 'mem')]
    pallas_call x0 -> x1, Pallas kernels: none -> 85.9 us  [per_device(): pl.pallas_call(kernel, out_shape=(jax.ShapeDtypeStruct((nodes, H), BF16),...]
    psum x1 -> x0, waiting for transfers between devices: 76.3 us -> none  [per_device(): weight_grad, bias_grad = lax.psum((local_grad, local_bias), ('grp', 'mem'))]
    while x40 -> x0, local copies, waits for them, and re-layouts: 58.4 us -> none
    all_gather x1 -> x0, waiting for transfers between devices: 57.1 us -> none  [per_device(): group = lax.all_gather(history, 'mem', axis=0, tiled=True)]
    dynamic_slice x20 -> x0, local copies, waits for them, and re-layouts: 15.7 us -> none  [the longest x10 8.13 us: accumulate(): rows = lax.dynamic_slice_in_dim(tile_row, start, step, 0)]
    reshape x2, local copies, waits for them, and re-layouts: 16.7 us -> 2.53 us  [the longest x1 1.27 us: per_device(): tile_row.reshape(1, TILES)]
  transfers between devices with their start and end apart: 2 -> 0, of which waited for: 2 -> 0; matrix products, arithmetic and copies ran while one was open for 0% -> 0% of each run, Pallas kernels for 0% -> 0%
where the time goes in v1:
time: 93.9 us; the launch traced here: 93.6 us
  Pallas kernels  85.9 us (91%)
  local copies, waits for them, and re-layouts  7.07 us (8%)
    pallas_call x1, Pallas kernels, per_device(): pl.pallas_call(kernel, out_shape=(jax.ShapeDtypeStruct((nodes, H), BF16),...  85.9 us
    unnamed x3, local copies, waits for them, and re-layouts  4.54 us

profile of v1, /device:TPU:1, one launch (start us, length us, event | category | flops | bytes accessed | tf_op | source)
XLA Modules:
  0.0 93.6 jit_solution(16177514077777250279)
XLA Ops:
  0.6 1.3 %reshape.22.row = s32[1,640]{1,0:T(1,128)} reshape(s32[640]{0:T(1024)} %param.9) | data formatting | bytes 5120 | tf_op jit(solution)/shard_map/reshape | solution.py:422
  1.9 1.3 %reshape.23.col = s32[1,640]{1,0:T(1,128)} reshape(s32[640]{0:T(1024)} %param.10) | data formatting | bytes 5120 | tf_op jit(solution)/shard_map/reshape | solution.py:423
  3.2 85.9 %shard_map.94 = (bf16[512,256]{1,0:T(8,128)(2,1)}, f32[256,256]{1,0:T(8,128)}, f32[1,256]{1,0:T(1,128)}) custom-call(bf16[4,128,256]{2,1,0:T(8,128)(2,1)} %bitcast.3, bf16[640,128,128]{2,1,0:T(8,128)(2,1)} %tiles.1, s32[1,640]{1,0:T(1,128)} %reshape.22.row, s32[1,640]{1,0:T(1,128)} %reshape.23.col, bf16[256,256]{1,0:T(8,128)(2,1)} %weight.1, ...), custom_call_target="tpu_custom_call" | custom-call | tf_op jit(solution)/shard_map/pallas_call | solution.py:378
  89.1 1.7 %copy.13 = bf16[512,256]{1,0:T(8,128)(2,1)} copy(bf16[512,256]{1,0:T(8,128)(2,1)} %get-tuple-element.12) | data formatting | bytes 524288
  90.7 1.7 %copy.14 = f32[256,256]{1,0:T(8,128)} copy(f32[256,256]{1,0:T(8,128)} %get-tuple-element.13) | data formatting | bytes 524288
  92.4 1.2 %copy.15 = f32[256]{0:T(256)} copy(f32[256]{0:T(256)} %bitcast.5) | data formatting | bytes 2048

commit v2 on v1

--- a/solution.py
+++ b/solution.py
@@ -135,6 +135,8 @@
         pl.semaphore_signal(barrier, inc=1, device_id={"mem": o}, device_id_type=MESH)
     for o in grp_others:
         pl.semaphore_signal(barrier, inc=1, device_id={"grp": o}, device_id_type=MESH)
+    for c in keep:
+        c.start()
     pl.semaphore_wait(barrier, MEM - 1 + GRP - 1)
 
     sends = []
@@ -175,8 +177,6 @@
     for j in range(OWN):
         for side in (1, -1):
             send(j, 0, 0, 1, side)
-    for c in keep:
-        c.start()
     load_tiles.start()
     load_w.start()
     load_cot.start()
@@ -188,7 +188,7 @@
         arrive(j, -matched(j), 0)
         pass_on(j, -matched(j), 0)
 
-    sort_tiles(row[...], col[...], order_v, ends_v)
+    sort_tiles(row[...].reshape(1, TILES), col[...].reshape(1, TILES), order_v, ends_v)
     to_s = [
         pltpu.make_async_copy(order_v, order_s, local_sem.at[7]),
         pltpu.make_async_copy(ends_v, ends_s, local_sem.at[8]),
@@ -222,8 +222,6 @@
     for df in (0, 1, -1, 2):
         for j in range(OWN):
             arrive(j, df, 2)
-    for c in sends:
-        c.wait_send()
 
     def product(slot):
         left = [tbuf[order_s[0, 2 * slot + k]] for k in (0, 1)]
@@ -245,6 +243,8 @@
         return 0
 
     lax.fori_loop(0, PAIRS // UNROLL, batch, 0)
+    for c in sends:
+        c.wait_send()
 
     own = hbuf
     sums = []
@@ -364,10 +364,16 @@
         c.wait_send()
     for c in third:
         c.wait_recv()
-    for m in range(MEM):
-        wgrad[m * PIECE : (m + 1) * PIECE, :] = got3[m].astype(F32)
+    wgrad[...] = got3[...]
     for c in third:
         c.wait_send()
+
+
+def finish(act, pieces, bgrad, act_out, wgrad_out, bgrad_out):
+    act_out[...] = act[...]
+    for m in range(MEM):
+        wgrad_out[m * PIECE : (m + 1) * PIECE, :] = pieces[m].astype(F32)
+    bgrad_out[...] = bgrad[...]
 
 
 def per_device(history, tiles, tile_row, tile_col, weight, bias, cotangent):
@@ -379,7 +385,7 @@
         kernel,
         out_shape=(
             jax.ShapeDtypeStruct((nodes, H), BF16),
-            jax.ShapeDtypeStruct((H, H), F32),
+            jax.ShapeDtypeStruct((MEM, PIECE, H), BF16),
             jax.ShapeDtypeStruct((1, H), F32),
         ),
         in_specs=[any_ref, any_ref, vmem, vmem, any_ref, vmem, any_ref],
@@ -419,12 +425,23 @@
     )(
         history.reshape(OWN, BS, H),
         tiles,
-        tile_row.reshape(1, TILES),
-        tile_col.reshape(1, TILES),
+        tile_row,
+        tile_col,
         weight,
         bias.reshape(1, H),
         cotangent,
     )
+    act, wgrad, bgrad = pl.pallas_call(
+        finish,
+        out_shape=(
+            jax.ShapeDtypeStruct((nodes, H), BF16),
+            jax.ShapeDtypeStruct((H, H), F32),
+            jax.ShapeDtypeStruct((1, H), F32),
+        ),
+        in_specs=[vmem, vmem, vmem],
+        out_specs=(vmem, vmem, vmem),
+        compiler_params=pltpu.CompilerParams(vmem_limit_bytes=61 * 2**20),
+    )(act, wgrad, bgrad)
     return act, wgrad, bgrad.reshape(H)
 
 

time: 93.9 us -> 88.6 us (0.944)
  local copies, waits for them, and re-layouts: 7.07 us -> 0 us
  Pallas kernels: 85.9 us -> 87.8 us
    unnamed x3 -> x0, local copies, waits for them, and re-layouts: 4.54 us -> none
    reshape x2 -> x0, local copies, waits for them, and re-layouts: 2.53 us -> none  [the longest x1 1.27 us: per_device(): tile_row.reshape(1, TILES)]
    pallas_call x0 -> x1, Pallas kernels: none -> 1.84 us  [per_device(): pl.pallas_call(finish, out_shape=(jax.ShapeDtypeStruct((nodes, H), BF16),...]
where the time goes in v2:
time: 88.6 us; the launch traced here: 88.4 us
  Pallas kernels  87.8 us (99%)
    pallas_call x1, Pallas kernels, per_device(): pl.pallas_call(kernel, out_shape=(jax.ShapeDtypeStruct((nodes, H), BF16),...  85.9 us
    pallas_call x1, Pallas kernels, per_device(): pl.pallas_call(finish, out_shape=(jax.ShapeDtypeStruct((nodes, H), BF16),...  1.84 us

profile of v2, /device:TPU:1, one launch (start us, length us, event | category | flops | bytes accessed | tf_op | source)
XLA Modules:
  0.0 88.4 jit_solution(14709931500558786288)
XLA Ops:
  0.6 85.9 %shard_map.94 = (bf16[512,256]{1,0:T(8,128)(2,1)}, bf16[16,16,256]{2,1,0:T(8,128)(2,1)}, f32[1,256]{1,0:T(1,128)}) custom-call(bf16[4,128,256]{2,1,0:T(8,128)(2,1)} %bitcast.3, bf16[640,128,128]{2,1,0:T(8,128)(2,1)} %tiles.1, s32[640]{0:T(1024)} %row.1, s32[640]{0:T(1024)} %col.1, bf16[256,256]{1,0:T(8,128)(2,1)} %weight.1, f32[1,256]{1,0:T(1,128)} %bitcast.4, ...), custom_call_target="tpu_custom_call" | custom-call | tf_op jit(solution)/shard_map/pallas_call | solution.py:384
  86.6 1.8 %shard_map.95 = (bf16[512,256]{1,0:T(8,128)(2,1)}, f32[256,256]{1,0:T(8,128)}, f32[1,256]{1,0:T(1,128)}) custom-call(bf16[512,256]{1,0:T(8,128)(2,1)} %get-tuple-element.9.act, bf16[16,16,256]{2,1,0:T(8,128)(2,1)} %get-tuple-element.10.pieces, f32[1,256]{1,0:T(1,128)} %get-tuple-element.11.bgrad), custom_call_target="tpu_custom_call" | custom-call | tf_op jit(solution)/shard_map/pallas_call | solution.py:434

commit v3 on v2

--- a/solution.py
+++ b/solution.py
@@ -284,21 +284,17 @@
         copy.start()
         sums.append(copy)
 
-    for df in (2, 1, -1, 0):
-        for j in range(OWN):
-            reduce_block(j, df, 2)
-    for df in (2, 1, -1, 0):
-        for j in range(OWN):
-            reduce_block(j, df, -matched(j))
-    for df in (2, 1, -1, 0):
-        for j in range(OWN):
-            reduce_block(j, df, matched(j))
-    for j in range(OWN):
-        reduce_block(j, 2, 0)
-    for j in range(OWN):
-        reduce_block(j, -matched(j), 0)
-    for j in range(OWN):
-        reduce_block(j, matched(j), 0)
+    for near in (2, 1, -1, 0):
+        for j in range(OWN):
+            reduce_block(j, near if near == 2 else near * matched(j), 2)
+    for near in (2, 1, -1, 0):
+        for j in range(OWN):
+            reduce_block(j, near if near == 2 else near * matched(j), -matched(j))
+        for j in range(OWN):
+            reduce_block(j, near if near == 2 else near * matched(j), matched(j))
+        if near != 2:
+            for j in range(OWN):
+                reduce_block(j, {1: 2, -1: matched(j), 0: -matched(j)}[near], 0)
 
     grad_sum = jnp.zeros((H, H), F32)
     bias_sum = jnp.zeros((1, H), F32)

time: 88.6 us -> 85.5 us (0.965)
  Pallas kernels: 87.8 us -> 84.7 us
    pallas_call x1, Pallas kernels: 85.9 us -> 82.9 us  [per_device(): pl.pallas_call(kernel, out_shape=(jax.ShapeDtypeStruct((nodes, H), BF16),...]
where the time goes in v3:
time: 85.5 us; the launch traced here: 85.4 us
  Pallas kernels  84.7 us (99%)
    pallas_call x1, Pallas kernels, per_device(): pl.pallas_call(kernel, out_shape=(jax.ShapeDtypeStruct((nodes, H), BF16),...  82.9 us
    pallas_call x1, Pallas kernels, per_device(): pl.pallas_call(finish, out_shape=(jax.ShapeDtypeStruct((nodes, H), BF16),...  1.84 us

profile of v3, /device:TPU:1, one launch (start us, length us, event | category | flops | bytes accessed | tf_op | source)
XLA Modules:
  0.0 85.4 jit_solution(8279196639189190406)
XLA Ops:
  0.6 82.9 %shard_map.94 = (bf16[512,256]{1,0:T(8,128)(2,1)}, bf16[16,16,256]{2,1,0:T(8,128)(2,1)}, f32[1,256]{1,0:T(1,128)}) custom-call(bf16[4,128,256]{2,1,0:T(8,128)(2,1)} %bitcast.3, bf16[640,128,128]{2,1,0:T(8,128)(2,1)} %tiles.1, s32[640]{0:T(1024)} %row.1, s32[640]{0:T(1024)} %col.1, bf16[256,256]{1,0:T(8,128)(2,1)} %weight.1, f32[1,256]{1,0:T(1,128)} %bitcast.4, ...), custom_call_target="tpu_custom_call" | custom-call | tf_op jit(solution)/shard_map/pallas_call | solution.py:380
  83.5 1.8 %shard_map.95 = (bf16[512,256]{1,0:T(8,128)(2,1)}, f32[256,256]{1,0:T(8,128)}, f32[1,256]{1,0:T(1,128)}) custom-call(bf16[512,256]{1,0:T(8,128)(2,1)} %get-tuple-element.9.act, bf16[16,16,256]{2,1,0:T(8,128)(2,1)} %get-tuple-element.10.pieces, f32[1,256]{1,0:T(1,128)} %get-tuple-element.11.bgrad), custom_call_target="tpu_custom_call" | custom-call | tf_op jit(solution)/shard_map/pallas_call | solution.py:430
